TPU v7x, 32 devices: a whole 2x2x4 slice. The times are simulated.
32 devices in a mesh: groups: 1, tp: 32 (over z, y, x, core).
Axes of the slice: x: 2, y: 2, z: 4, core: 2. Of those that a mesh axis runs over, the one named last changes fastest.
Arguments:
- hidden_in: bfloat16 [192, 3584], P(('groups', 'tp')), may hold values from -6 to 6
- norm_dense: float32 [3584], replicated, may hold values from 0.1 to 1.9
- dense_gate: bfloat16 [3584, 18432], P(None, 'tp'), may hold values from -0.09375 to 0.09375
- dense_up: bfloat16 [3584, 18432], P(None, 'tp'), may hold values from -0.09375 to 0.09375
- dense_down: bfloat16 [18432, 3584], P('tp'), may hold values from -0.046875 to 0.046875
- norm_moe: float32 [3584], replicated, may hold values from 0.1 to 1.9
- expert_gate: bfloat16 [32, 3584, 256], P('tp'), may hold values from -0.09375 to 0.09375
- expert_up: bfloat16 [32, 3584, 256], P('tp'), may hold values from -0.09375 to 0.09375
- expert_down: bfloat16 [32, 256, 3584], P('tp'), may hold values from -0.1875 to 0.1875
- expert_ids: int32 [192, 4], P(('groups', 'tp')), may hold values from 0 to 7, all different within a row; in each aligned block of 6 rows (0 to 5, 6 to 11, ...) at most 4 rows name the same one
- gate_weights: float32 [192, 4], P(('groups', 'tp')), may hold values from 0.1 to 1
- placement: int32 [32], replicated, may hold values from 0 to 31, each once
- request_counts: int32 [32], P('groups'), may hold values from 1 to 2, 42 in all
Outputs:
- layer_out: bfloat16 [192, 3584], P(('groups', 'tp'))
Inputs may be any that keep to these rules, and one draw needn't show every extreme that they name: `expert_ids`: in each aligned block of 6 rows (the rows of one device), no expert is named by more than 4 rows; some expert reaches 4 in some block. The 4 experts of a row differ. `placement`: A permutation: each device holds exactly one expert slice. `request_counts`: the counts of each group (serving replica) sum to 42; the largest is exactly 2.
All inputs are finite; a program needn't handle non-finite values.
Results may differ from a plain program's by a relative error of at most 0.0071.
Values may be sent and summed in bfloat16 or wider, within the bound.
A program may use at most 64 MiB of HBM per device.

v0:
```python
import jax
import jax.numpy as jnp
from jax import lax
from jax.sharding import PartitionSpec as P

SPLIT = 4
TOP = 4
DRAFT = 3


epsilon = 1e-06


def rms_scale(values, scale_gain):
    widened = values.astype(jnp.float32)
    return (
        widened
        * lax.rsqrt(jnp.mean(widened * widened, axis=-1, keepdims=True) + epsilon)
        * scale_gain
    )


def slot_table(named_rows, capacity):
    slot_rank = jnp.cumsum(named_rows.astype(jnp.int32), axis=1) - 1
    slot_ids = jnp.arange(capacity, dtype=jnp.int32)
    return named_rows[:, None, :] & (slot_rank[:, None, :] == slot_ids[None, :, None])


def body(
    hidden_in,
    norm_dense,
    dense_gate,
    dense_up,
    dense_down,
    norm_moe,
    expert_gate,
    expert_up,
    expert_down,
    expert_ids,
    gate_weights,
    placement,
    request_counts,
):
    rows_dev = hidden_in.shape[0]
    feature_dim = hidden_in.shape[1]
    devices = lax.axis_size("tp")
    myself = lax.axis_index("tp")
    experts = devices // SPLIT
    capacity = min(rows_dev, 3 * ((rows_dev * TOP + experts - 1) // experts) // 2)
    device_ids = jnp.arange(devices, dtype=jnp.int32)
    hosted_slot = jnp.sum(
        jnp.where(placement[None, :] == device_ids[:, None], device_ids[None, :], 0), axis=1
    )
    hosted_expert = hosted_slot // SPLIT
    my_count = jnp.sum(jnp.where(device_ids == myself, request_counts, 0))
    live_rows = jnp.arange(rows_dev, dtype=jnp.int32) < DRAFT * my_count
    named_match = expert_ids[None, :, :] == hosted_expert[:, None, None]
    own_slots = slot_table(jnp.any(named_match, axis=2), capacity)
    normed = rms_scale(lax.all_gather(hidden_in, "tp", axis=0, tiled=True), norm_dense).astype(
        jnp.bfloat16
    )
    gate_proj = jnp.dot(normed, dense_gate, preferred_element_type=jnp.float32)
    up_proj = jnp.dot(normed, dense_up, preferred_element_type=jnp.float32)
    inner_act = (jax.nn.silu(gate_proj) * up_proj).astype(jnp.bfloat16)
    partial_value = jnp.dot(inner_act, dense_down, preferred_element_type=jnp.float32)
    dense_sum = lax.psum_scatter(partial_value, "tp", scatter_dimension=0, tiled=True)
    mixed_rows = (hidden_in.astype(jnp.float32) + dense_sum).astype(jnp.bfloat16)
    routed = rms_scale(mixed_rows, norm_moe).astype(jnp.bfloat16)
    send_rows = jnp.einsum(
        "dcr,rf->dcf", own_slots.astype(jnp.bfloat16), routed, preferred_element_type=jnp.float32
    ).astype(jnp.bfloat16)
    received = lax.all_to_all(send_rows, "tp", split_axis=0, concat_axis=0, tiled=True)
    slot_count = received.shape[1]
    flat_rows = received.reshape(devices * slot_count, feature_dim)
    gate_proj = jnp.dot(flat_rows, expert_gate[0], preferred_element_type=jnp.float32)
    up_proj = jnp.dot(flat_rows, expert_up[0], preferred_element_type=jnp.float32)
    inner_act = (jax.nn.silu(gate_proj) * up_proj).astype(jnp.bfloat16)
    partial_out = jnp.dot(inner_act, expert_down[0], preferred_element_type=jnp.float32).astype(
        jnp.bfloat16
    )
    returned_rows = lax.all_to_all(
        partial_out.reshape(devices, slot_count, feature_dim),
        "tp",
        split_axis=0,
        concat_axis=0,
        tiled=True,
    )
    row_weight = jnp.sum(jnp.where(named_match, gate_weights[None, :, :], 0.0), axis=2)
    combine_coef = jnp.where(own_slots, row_weight[:, None, :], 0.0)
    routed_sum = jnp.einsum(
        "dcr,dcf->rf",
        combine_coef,
        returned_rows.astype(jnp.float32),
        precision=lax.Precision.HIGHEST,
    )
    result = (mixed_rows.astype(jnp.float32) + routed_sum).astype(jnp.bfloat16)
    return jnp.where(live_rows[:, None], result, jnp.zeros_like(result))


def solution(mesh):
    in_specs = (
        P(("groups", "tp"), None),
        P(),
        P(None, "tp"),
        P(None, "tp"),
        P("tp", None),
        P(),
        P("tp", None, None),
        P("tp", None, None),
        P("tp", None, None),
        P(("groups", "tp"), None),
        P(("groups", "tp"), None),
        P(),
        P("groups"),
    )
    out_specs = P(("groups", "tp"), None)
    return jax.shard_map(body, mesh=mesh, in_specs=in_specs, out_specs=out_specs, check_vma=False)
```

profile of v0, /device:TPU:0, one launch (start us, length us, event | category | flops | bytes accessed | tf_op | source)
XLA Modules:
  0.0 270.3 jit_solution(6328504494341048749)
XLA Ops:
  7.3 0.8 select_reduce_fusion
  8.0 60.7 %all-gather.3.cloned.1.call-done = bf16[32,6,3584]{2,1,0:T(8,128)(2,1)} async-done(((bf16[1,6,3584]{2,1,0:T(8,128)(2,1)}), bf16[32,6,3584]{2,1,0:T(8,128)(2,1)}) %all-gather.3.cloned.1.call-update) | async-done | bytes 1376272 | tf_op jit(solution)/shard_map/all_gather | solution.py:59
  68.7 3.6 %reshape.63 = f32[192,3584]{1,0:T(8,128)} reshape(bf16[32,6,3584]{2,1,0:T(8,128)(2,1)} %all-gather.3.cloned.1.call-done) | data formatting | bytes 4128768 | tf_op jit(solution)/shard_map/convert_element_type | solution.py:15
  72.3 2.2 multiply_reduce_fusion
  74.9 3.8 %fusion.55 = f32[192,576]{1,0:T(8,128)S(1)} fusion(bf16[3584,576]{0,1:T(8,128)(2,1)} %param.15, f32[192,3584]{1,0:T(8,128)S(1)} %copy-done.1, f32[3584]{0:T(1024)S(1)} %copy-done.6, f32[192]{0:T(256)S(1)} %add_rsqrt_fusion), kind=kOutput, calls=%fused_computation.68 | convolution fusion | flops 794787840 | bytes 7338752 | tf_op jit(solution)/shard_map/dot_general | solution.py:62
  78.7 9.2 %fusion.19 = f32[192,3584]{1,0:T(8,128)} fusion(bf16[576,3584]{1,0:T(8,128)(2,1)} %param.17, bf16[3584,576]{0,1:T(8,128)(2,1)} %param.16, f32[192,576]{1,0:T(8,128)S(1)} %fusion.55, f32[192,3584]{1,0:T(8,128)} %reshape.63, f32[3584]{0:T(1024)S(1)} %copy-done.6, f32[192]{0:T(256)S(1)} %add_rsqrt_fusion), kind=kOutput, calls=%fused_computation.18 | convolution fusion | flops 1588174848 | bytes 14220032 | tf_op jit(solution)/shard_map/dot_general | solution.py:65
  87.9 82.4 %fusion = f32[8,3584]{1,0:T(8,128)S(1)} fusion(f32[192,3584]{1,0:T(8,128)} %fusion.19), kind=kCustom, calls=%all-reduce-scatter | all-reduce-scatter fusion | flops 917505 | bytes 2867200
  170.3 1.3 collective-permute-start
  171.6 1.3 collective-permute-start.1
  173.0 1.3 collective-permute-start.7
  174.5 1.3 collective-permute-start.2
  175.8 1.3 collective-permute-start.3
  177.1 1.3 collective-permute-start.4
  178.4 5.5 %collective-permute-start.5 = (f32[8,3584]{1,0:T(8,128)S(1)}, f32[8,3584]{1,0:T(8,128)S(1)}, u32[]{:S(2)}, u32[]{:S(2)}) collective-permute-start(f32[8,3584]{1,0:T(8,128)S(1)} %fusion), channel_id=1, source_target_pairs={{0,6},{1,7},{2,8},{3,9},{4,10},{5,11},{6,12},{7,13},{8,14},{9,15},... | collective-permute-start | bytes 344072
  183.9 6.1 %collective-permute-start.6 = (f32[8,3584]{1,0:T(8,128)S(1)}, f32[8,3584]{1,0:T(8,128)}, u32[]{:S(2)}, u32[]{:S(2)}) collective-permute-start(f32[8,3584]{1,0:T(8,128)S(1)} %fusion), channel_id=1, source_target_pairs={{0,7},{1,8},{2,9},{3,10},{4,11},{5,12},{6,13},{7,14},{8,15},{9,16}... | collective-permute-start | bytes 344072
  191.8 4.9 %concatenate = f32[70,3584]{1,0:T(8,128)S(1)} concatenate(f32[6,3584]{1,0:T(8,128)S(1)} %collective-permute-done.7, f32[8,3584]{1,0:T(8,128)} %collective-permute-done.6, f32[8,3584]{1,0:T(8,128)} %copy-done.5, f32[8,3584]{1,0:T(8,128)} %copy-done.4, f32[8,3584]{1,0:T(8,128)} %copy-done.3, f32[8,3584]{1,0:T(8,128)S(1)} %collective-permute-done.2, ...), dimensions={0} | concatenate | bytes 2007040
  198.1 27.4 %all_to_all.10 = bf16[32,4,3584]{2,1,0:T(4,128)(2,1)} all-to-all(bf16[32,4,3584]{2,1,0:T(4,128)(2,1)S(1)} %copy.27), channel_id=1, replica_groups=mesh['groups'=1,'tp'=32] {'tp'}, dimensions={0} | all-to-all | bytes 1835008 | tf_op jit(solution)/shard_map/all_to_all | solution.py:72
  225.5 1.7 reshape.59
  227.2 1.9 fusion.7
  229.1 3.6 %convolution_convert_fusion = bf16[128,3584]{1,0:T(8,128)(2,1)} fusion(bf16[1,256,3584]{2,1,0:T(8,128)(2,1)S(1)} %copy-done, bf16[128,3584]{1,0:T(8,128)(2,1)S(1)} %reshape.59, bf16[1,3584,256]{2,1,0:T(8,128)(2,1)} %param.20, f32[128,256]{1,0:T(8,128)S(1)} %fusion.7), kind=kOutput, calls=%fused_computation | convolution fusion | flops 470417408 | bytes 5636096 | tf_op jit(solution)/shard_map/dot_general | solution.py:78
  232.7 2.5 reshape.60
  235.2 3.6 %all-to-all-start.1 = ((bf16[32,4,3584]{2,1,0:T(4,128)(2,1)}), bf16[32,4,3584]{2,1,0:T(4,128)(2,1)S(1)}, u32[]{:S(2)}, u32[]{:S(2)}) async-start(bf16[32,4,3584]{2,1,0:T(4,128)(2,1)} %reshape.60), calls=%async_computation.1 | async-start | bytes 1835008 | tf_op jit(solution)/shard_map/all_to_all | solution.py:81
  240.4 21.9 %all-to-all-done.1 = bf16[32,4,3584]{2,1,0:T(4,128)(2,1)S(1)} async-done(((bf16[32,4,3584]{2,1,0:T(4,128)(2,1)}), bf16[32,4,3584]{2,1,0:T(4,128)(2,1)S(1)}, u32[]{:S(2)}, u32[]{:S(2)}) %all-to-all-start.1) | async-done | bytes 917536 | tf_op jit(solution)/shard_map/all_to_all | solution.py:81
  262.3 1.2 fusion.3
  (48 shorter events, 5.2 us)
Async XLA Ops:
  6.5 222.5 %copy-start = (bf16[1,256,3584]{2,1,0:T(8,128)(2,1)S(1)}, bf16[1,256,3584]{2,1,0:T(8,128)(2,1)}, u32[]{:S(2)}) copy-start(bf16[1,256,3584]{2,1,0:T(8,128)(2,1)} %param.21) | copy-start | bytes 5505028
  6.5 62.2 %all-gather.3.cloned.1.call-start = ((), (), s32[]{:S(2)}) async-start(), calls=%async_computation.2 | async-start | bytes 1892352 | tf_op jit(solution)/shard_map/all_gather | solution.py:59
  8.0 66.5 %copy-start.6 = (f32[3584]{0:T(1024)S(1)}, f32[3584]{0:T(1024)}, u32[]{:S(2)}) copy-start(f32[3584]{0:T(1024)} %param.14) | copy-start | bytes 43012
  72.3 2.6 copy-start.1
  87.9 85.0 %copy-start.8 = (s32[6,4]{0,1:T(4,128)S(1)}, s32[6,4]{0,1:T(4,128)}, u32[]{:S(2)}) copy-start(s32[6,4]{0,1:T(4,128)} %param.22) | copy-start | bytes 292
  87.9 108.8 %copy-start.2 = (bf16[6,3584]{1,0:T(8,128)(2,1)S(1)}, bf16[6,3584]{1,0:T(8,128)(2,1)}, u32[]{:S(2)}) copy-start(bf16[6,3584]{1,0:T(8,128)(2,1)} %param.13) | copy-start | bytes 129028
  87.9 109.0 %copy-start.7 = (f32[3584]{0:T(1024)S(1)}, f32[3584]{0:T(1024)}, u32[]{:S(2)}) copy-start(f32[3584]{0:T(1024)} %param.18) | copy-start | bytes 43012
  170.3 8.1 %collective-permute-start = (f32[8,3584]{1,0:T(8,128)S(1)}, f32[8,3584]{1,0:T(8,128)S(1)}, u32[]{:S(2)}, u32[]{:S(2)}) collective-permute-start(f32[8,3584]{1,0:T(8,128)S(1)} %fusion), channel_id=1, source_target_pairs={{0,1},{1,2},{2,3},{3,4},{4,5},{5,6},{6,7},{7,8},{8,9},{9,10},{10,1... | collective-permute-start | bytes 344072
  171.6 12.3 %collective-permute-start.1 = (f32[8,3584]{1,0:T(8,128)S(1)}, f32[8,3584]{1,0:T(8,128)S(1)}, u32[]{:S(2)}, u32[]{:S(2)}) collective-permute-start(f32[8,3584]{1,0:T(8,128)S(1)} %fusion), channel_id=1, source_target_pairs={{0,2},{1,3},{2,4},{3,5},{4,6},{5,7},{6,8},{7,9},{8,10},{9,11},{10,... | collective-permute-start | bytes 344072
  173.0 4.0 %collective-permute-start.7 = (f32[6,3584]{1,0:T(8,128)S(1)}, f32[6,3584]{1,0:T(8,128)S(1)}, u32[]{:S(2)}, u32[]{:S(2)}) collective-permute-start(f32[6,3584]{1,0:T(8,128)S(1)} %slice), channel_id=1, source_target_pairs={{0,8},{1,9},{2,10},{3,11},{4,12},{5,13},{6,14},{7,15},{8,16},{9,17... | collective-permute-start | bytes 258056
  174.5 15.6 %collective-permute-start.2 = (f32[8,3584]{1,0:T(8,128)S(1)}, f32[8,3584]{1,0:T(8,128)S(1)}, u32[]{:S(2)}, u32[]{:S(2)}) collective-permute-start(f32[8,3584]{1,0:T(8,128)S(1)} %fusion), channel_id=1, source_target_pairs={{0,3},{1,4},{2,5},{3,6},{4,7},{5,8},{6,9},{7,10},{8,11},{9,12},{10... | collective-permute-start | bytes 344072
  175.8 14.3 %collective-permute-start.3 = (f32[8,3584]{1,0:T(8,128)S(1)}, f32[8,3584]{1,0:T(8,128)S(1)}, u32[]{:S(2)}, u32[]{:S(2)}) collective-permute-start(f32[8,3584]{1,0:T(8,128)S(1)} %fusion), channel_id=1, source_target_pairs={{0,4},{1,5},{2,6},{3,7},{4,8},{5,9},{6,10},{7,11},{8,12},{9,13},{1... | collective-permute-start | bytes 344072
  177.1 13.0 %collective-permute-start.4 = (f32[8,3584]{1,0:T(8,128)S(1)}, f32[8,3584]{1,0:T(8,128)S(1)}, u32[]{:S(2)}, u32[]{:S(2)}) collective-permute-start(f32[8,3584]{1,0:T(8,128)S(1)} %fusion), channel_id=1, source_target_pairs={{0,5},{1,6},{2,7},{3,8},{4,9},{5,10},{6,11},{7,12},{8,13},{9,14},{... | collective-permute-start | bytes 344072
  178.4 11.7 %collective-permute-start.5 = (f32[8,3584]{1,0:T(8,128)S(1)}, f32[8,3584]{1,0:T(8,128)S(1)}, u32[]{:S(2)}, u32[]{:S(2)}) collective-permute-start(f32[8,3584]{1,0:T(8,128)S(1)} %fusion), channel_id=1, source_target_pairs={{0,6},{1,7},{2,8},{3,9},{4,10},{5,11},{6,12},{7,13},{8,14},{9,15},... | collective-permute-start | bytes 344072
  183.9 7.8 %collective-permute-start.6 = (f32[8,3584]{1,0:T(8,128)S(1)}, f32[8,3584]{1,0:T(8,128)}, u32[]{:S(2)}, u32[]{:S(2)}) collective-permute-start(f32[8,3584]{1,0:T(8,128)S(1)} %fusion), channel_id=1, source_target_pairs={{0,7},{1,8},{2,9},{3,10},{4,11},{5,12},{6,13},{7,14},{8,15},{9,16}... | collective-permute-start | bytes 344072
  190.1 0.6 copy-start.3
  190.1 0.7 copy-start.4
  190.7 0.6 copy-start.5
  232.7 6.2 %copy-start.9 = (f32[6,4]{0,1:T(4,128)S(1)}, f32[6,4]{0,1:T(4,128)}, u32[]{:S(2)}) copy-start(f32[6,4]{0,1:T(4,128)} %param.23) | copy-start | bytes 292
  232.7 6.3 %copy-start.10 = (s32[32]{0:T(128)S(1)}, s32[32]{0:T(128)}, u32[]{:S(2)}) copy-start(s32[32]{0:T(128)} %param.25) | copy-start | bytes 388
  235.2 27.1 %all-to-all-start.1 = ((bf16[32,4,3584]{2,1,0:T(4,128)(2,1)}), bf16[32,4,3584]{2,1,0:T(4,128)(2,1)S(1)}, u32[]{:S(2)}, u32[]{:S(2)}) async-start(bf16[32,4,3584]{2,1,0:T(4,128)(2,1)} %reshape.60), calls=%async_computation.1 | async-start | bytes 1835008 | tf_op jit(solution)/shard_map/all_to_all | solution.py:81
Sparse Core Ops, SparseCore 0:
  10.2 58.4 all-gather.2
where the time goes:
time: 271 us; the launch traced here: 270 us
  blocking collectives  110 us (41%)
  waiting for transfers between devices  83.7 us (31%)
  starting transfers between devices  23 us (8%)
  matrix products  20.2 us (7%)
  local copies, waits for them, and re-layouts  15.3 us (6%)
  between operations  14.3 us (5%)
  other arithmetic  3.99 us (1%)
    unnamed x1, blocking collectives  82.4 us
    all_gather x1, waiting for transfers between devices, body(): lax.all_gather(hidden_in, 'tp', axis=0, tiled=True)  60.7 us
    all_to_all x1, blocking collectives, body(): lax.all_to_all(send_rows, 'tp', split_axis=0, concat_axis=0, tiled=True)  27.4 us
    all_to_all x1, waiting for transfers between devices, body(): lax.all_to_all(partial_out.reshape(devices, slot_count, feature_dim), 'tp...  21.9 us
    unnamed x8, starting transfers between devices  19.4 us
    dot_general x1, matrix products, body(): jnp.dot(inner_act, dense_down, preferred_element_type=jnp.float32)  9.17 us
    unnamed x26, local copies, waits for them, and re-layouts  6.86 us
  transfers between devices with their start and end apart: 10, of which 3 were waited for; matrix products, arithmetic and copies ran while one was open for 1% of the time, Pallas kernels for 0%

commit v1 on v0

v1 whole, which is shorter than its diff:
```python
import functools

import jax
import jax.numpy as jnp
from jax import lax
from jax.experimental import pallas as pl
from jax.experimental.pallas import tpu as pltpu
from jax.sharding import PartitionSpec as P

SPLIT = 4
TOP = 4
DRAFT = 3
PAD = 8
HALF = 64
LANES = 128

epsilon = 1e-06


def rms_scale(widened, scale_gain):
    return (
        widened
        * lax.rsqrt(jnp.mean(widened * widened, axis=-1, keepdims=True) + epsilon)
        * scale_gain
    )


def kernel(
    n,
    hid,
    gain1,
    wg_hbm,
    wu_hbm,
    wd_hbm,
    gain2,
    eg_hbm,
    eu_hbm,
    ed_hbm,
    ids,
    gws,
    place,
    counts,
    out,
    wg,
    wu,
    wd,
    eg,
    eu,
    ed,
    pad_ref,
    mixed_ref,
    buf1,
    buf2,
    x2d,
    acc_g,
    acc_u,
    inner,
    acc_eg,
    acc_eu,
    inner_e,
    part,
    sbuf1,
    sbuf2,
    rbuf1,
    rbuf2,
    wsem,
    ssem,
    rsem,
):
    Z = n // 8
    rows = hid.shape[0]
    D = hid.shape[1]
    me = lax.axis_index("tp")
    c = lax.rem(me, 2)
    x = lax.rem(lax.div(me, 2), 2)
    y = lax.rem(lax.div(me, 4), 2)
    z = lax.div(me, 8)
    c_dev = me + 1 - 2 * c
    x_dev = me + 2 - 4 * x
    y_dev = me + 4 - 8 * y
    z_devs = [None] + [me + 8 * (lax.rem(z + j, Z) - z) for j in range(1, Z)]
    partners = [c_dev, x_dev, y_dev] + z_devs[1:]

    loads = [
        pltpu.make_async_copy(src, dst, wsem.at[i])
        for i, (src, dst) in enumerate(
            [
                (wg_hbm, wg),
                (wu_hbm, wu),
                (wd_hbm, wd),
                (eg_hbm.at[0], eg),
                (eu_hbm.at[0], eu),
                (ed_hbm.at[0], ed),
            ]
        )
    ]

    barrier = pltpu.get_barrier_semaphore()
    for dev in partners:
        pl.semaphore_signal(
            barrier, inc=1, device_id={"tp": dev}, device_id_type=pl.DeviceIdType.MESH
        )
    for load in loads:
        load.start()

    hidden = hid[...].astype(jnp.float32)
    pad_ref[...] = jnp.zeros_like(pad_ref)
    pad_ref[0:rows, :] = rms_scale(hidden, gain1[...])
    buf1[0] = pad_ref[...].astype(jnp.bfloat16)
    pl.semaphore_wait(barrier, len(partners))

    def remote(phase, src, dst, k, dev):
        return pltpu.make_async_remote_copy(
            src_ref=src,
            dst_ref=dst,
            send_sem=ssem.at[phase, k],
            recv_sem=rsem.at[phase, k],
            device_id={"tp": dev},
            device_id_type=pl.DeviceIdType.MESH,
        )

    def gather(phase, buf):
        def send(k, slot, dev):
            remote(phase, buf.at[k], buf.at[slot], slot, dev).start()

        def arrived(k):
            remote(phase, buf.at[k], buf.at[k], k, c_dev).wait_recv()

        send(0, 2 * Z, x_dev)
        send(0, Z, y_dev)
        for j in range(1, Z):
            send(0, j, z_devs[j])
        send(0, 4 * Z, c_dev)

        @pl.loop(1, Z)
        def _(k):
            arrived(k)
            send(k, 2 * Z + k, x_dev)
            send(k, Z + k, y_dev)
            send(k, 4 * Z + k, c_dev)

        @pl.loop(Z, 2 * Z)
        def _(k):
            arrived(k)
            send(k, 2 * Z + k, x_dev)
            send(k, 4 * Z + k, c_dev)

        @pl.loop(2 * Z, 4 * Z)
        def _(k):
            arrived(k)
            send(k, 4 * Z + k, c_dev)

        @pl.loop(4 * Z, 8 * Z)
        def _(k):
            arrived(k)

    def scatter(phase, sbuf, rbuf):
        def send(k, dev):
            remote(phase, sbuf.at[k], rbuf.at[k], k, dev).start()

        def arrived(k):
            remote(phase, sbuf.at[k], rbuf.at[k], k, c_dev).wait_recv()
            return rbuf[k].astype(jnp.float32)

        def first(k):
            sbuf[k] = part[k].astype(jnp.bfloat16)
            send(k, c_dev)

        pl.loop(6 * Z, 8 * Z)(first)
        pl.loop(5 * Z, 6 * Z)(first)
        pl.loop(4 * Z, 5 * Z)(first)

        @pl.loop(2 * Z, 4 * Z)
        def _(k):
            total = part[k] + arrived(4 * Z + k)
            sbuf[k] = total.astype(jnp.bfloat16)
            send(k, x_dev)

        @pl.loop(Z, 2 * Z)
        def _(k):
            total = part[k] + arrived(4 * Z + k) + arrived(2 * Z + k)
            sbuf[k] = total.astype(jnp.bfloat16)
            send(k, y_dev)

        for k in range(1, Z):
            total = part[k] + arrived(4 * Z + k) + arrived(2 * Z + k) + arrived(Z + k)
            sbuf[k] = total.astype(jnp.bfloat16)
            send(k, z_devs[Z - k])
        total = part[0] + arrived(4 * Z) + arrived(2 * Z) + arrived(Z)
        for k in range(1, Z):
            total = total + arrived(k)
        return total

    def flatten(buf):
        @pl.loop(0, n // 4)
        def _(b):
            block = buf[pl.ds(b * 4, 4), :, 0:D].astype(jnp.float32)
            x2d[pl.ds(pl.multiple_of(b * 4 * PAD, 4 * PAD), 4 * PAD), :] = block.reshape(
                4 * PAD, D
            ).astype(jnp.bfloat16)

    def project(gate_w, up_w, gate_acc, up_acc, result):
        step = 512
        gate_acc[...] = jnp.zeros_like(gate_acc)
        up_acc[...] = jnp.zeros_like(up_acc)

        @pl.loop(0, D // step)
        def _(i):
            span = pl.ds(pl.multiple_of(i * step, step), step)
            left = x2d[:, span]
            gate_acc[...] += jnp.dot(left, gate_w[span, :], preferred_element_type=jnp.float32)
            up_acc[...] += jnp.dot(left, up_w[span, :], preferred_element_type=jnp.float32)

        gate = gate_acc[...]
        result[...] = (gate / (1.0 + jnp.exp(-gate)) * up_acc[...]).astype(jnp.bfloat16)

    def down(act, down_w, scale):
        step = 512

        @pl.loop(0, D // step)
        def _(i):
            span = pl.ds(pl.multiple_of(i * step, step), step)
            value = jnp.dot(act[...], down_w[:, span], preferred_element_type=jnp.float32)
            value = value.reshape(n, PAD, step)
            part[:, :, span] = value if scale is None else value * scale

    gather(0, buf1)
    flatten(buf1)
    loads[0].wait()
    loads[1].wait()
    project(wg, wu, acc_g, acc_u, inner)
    loads[2].wait()
    down(inner, wd, None)
    dense_sum = scatter(1, sbuf1, rbuf1)

    mixed = (hid[...].astype(jnp.float32) + dense_sum[0:rows]).astype(jnp.bfloat16)
    mixed = mixed.astype(jnp.float32)
    mixed_ref[...] = mixed
    pad_ref[0:rows, :] = rms_scale(mixed, gain2[...])
    buf2[0, :, 0:D] = pad_ref[...].astype(jnp.bfloat16)
    lane = lax.broadcasted_iota(jnp.int32, (rows, LANES), 1)
    expert = lax.rem(lane, HALF)
    weight = jnp.zeros((rows, LANES), jnp.float32)
    for k in range(TOP):
        weight = weight + jnp.where(ids[:, k : k + 1] == expert, gws[:, k : k + 1], 0.0)
    high = weight.astype(jnp.bfloat16).astype(jnp.float32)
    pad_ref[0:rows, 0:LANES] = jnp.where(lane < HALF, high, weight - high)
    buf2[0, :, D : D + LANES] = pad_ref[:, 0:LANES].astype(jnp.bfloat16)

    gather(2, buf2)
    flatten(buf2)
    loads[3].wait()
    loads[4].wait()
    project(eg, eu, acc_eg, acc_eu, inner_e)
    slot = lax.broadcasted_iota(jnp.int32, (1, n), 1)
    hosted = jnp.sum(
        jnp.where(place[...] == me, lax.div(slot, SPLIT), 0).astype(jnp.float32),
        axis=1,
        keepdims=True,
    )
    lane3 = lax.rem(lax.broadcasted_iota(jnp.int32, (1, LANES), 1), HALF)
    chosen = jnp.where(lane3.astype(jnp.float32) == hosted, 1.0, 0.0)
    row_weight = jnp.sum(
        buf2[:, :, D : D + LANES].astype(jnp.float32) * chosen[None], axis=2, keepdims=True
    )
    loads[5].wait()
    down(inner_e, ed, row_weight)
    routed_sum = scatter(3, sbuf2, rbuf2)

    count = jnp.sum(
        jnp.where(slot == me, counts[...], 0).astype(jnp.float32), axis=1, keepdims=True
    )
    row = lax.broadcasted_iota(jnp.int32, (rows, 1), 0).astype(jnp.float32)
    final = mixed_ref[...] + routed_sum[0:rows]
    out[...] = jnp.where(row < DRAFT * count, final, 0.0).astype(out.dtype)

    @pl.loop(1, n)
    def _(k):
        remote(0, buf1.at[k], buf1.at[k], k, c_dev).wait_send()
        remote(1, sbuf1.at[k], rbuf1.at[k], k, c_dev).wait_send()
        remote(2, buf2.at[k], buf2.at[k], k, c_dev).wait_send()
        remote(3, sbuf2.at[k], rbuf2.at[k], k, c_dev).wait_send()


def body(
    hidden_in,
    norm_dense,
    dense_gate,
    dense_up,
    dense_down,
    norm_moe,
    expert_gate,
    expert_up,
    expert_down,
    expert_ids,
    gate_weights,
    placement,
    request_counts,
):
    n = lax.axis_size("tp")
    D = hidden_in.shape[1]
    F = dense_gate.shape[1]
    E = expert_gate.shape[2]
    vmem = pl.BlockSpec(memory_space=pltpu.VMEM)
    hbm = pl.BlockSpec(memory_space=pl.ANY)
    bf16, f32 = jnp.bfloat16, jnp.float32
    total_rows = n * PAD
    return pl.pallas_call(
        functools.partial(kernel, n),
        out_shape=jax.ShapeDtypeStruct(hidden_in.shape, hidden_in.dtype),
        in_specs=[vmem, vmem, hbm, hbm, hbm, vmem, hbm, hbm, hbm, vmem, vmem, vmem, vmem],
        out_specs=vmem,
        scratch_shapes=[
            pltpu.VMEM((D, F), bf16),
            pltpu.VMEM((D, F), bf16),
            pltpu.VMEM((F, D), bf16),
            pltpu.VMEM((D, E), bf16),
            pltpu.VMEM((D, E), bf16),
            pltpu.VMEM((E, D), bf16),
            pltpu.VMEM((PAD, D), f32),
            pltpu.VMEM(hidden_in.shape, f32),
            pltpu.VMEM((n, PAD, D), bf16),
            pltpu.VMEM((n, PAD, D + LANES), bf16),
            pltpu.VMEM((total_rows, D), bf16),
            pltpu.VMEM((total_rows, F), f32),
            pltpu.VMEM((total_rows, F), f32),
            pltpu.VMEM((total_rows, F), bf16),
            pltpu.VMEM((total_rows, E), f32),
            pltpu.VMEM((total_rows, E), f32),
            pltpu.VMEM((total_rows, E), bf16),
            pltpu.VMEM((n, PAD, D), f32),
            pltpu.VMEM((n, PAD, D), bf16),
            pltpu.VMEM((n, PAD, D), bf16),
            pltpu.VMEM((n, PAD, D), bf16),
            pltpu.VMEM((n, PAD, D), bf16),
            pltpu.SemaphoreType.DMA((6,)),
            pltpu.SemaphoreType.DMA((4, n)),
            pltpu.SemaphoreType.DMA((4, n)),
        ],
        compiler_params=pltpu.CompilerParams(
            collective_id=0, has_side_effects=True, vmem_limit_bytes=60 * 1024 * 1024
        ),
    )(
        hidden_in,
        norm_dense.reshape(1, D),
        dense_gate,
        dense_up,
        dense_down,
        norm_moe.reshape(1, D),
        expert_gate,
        expert_up,
        expert_down,
        expert_ids,
        gate_weights,
        placement.reshape(1, n),
        request_counts.reshape(1, n),
    )


def solution(mesh):
    in_specs = (
        P(("groups", "tp"), None),
        P(),
        P(None, "tp"),
        P(None, "tp"),
        P("tp", None),
        P(),
        P("tp", None, None),
        P("tp", None, None),
        P("tp", None, None),
        P(("groups", "tp"), None),
        P(("groups", "tp"), None),
        P(),
        P("groups"),
    )
    out_specs = P(("groups", "tp"), None)
    return jax.shard_map(body, mesh=mesh, in_specs=in_specs, out_specs=out_specs, check_vma=False)
```

time: 271 us -> 109 us (0.40)
  blocking collectives: 110 us -> 0 us
  Pallas kernels: 0 us -> 88.6 us
  waiting for transfers between devices: 83.7 us -> 0 us
  starting transfers between devices: 23 us -> 0 us
  matrix products: 20.2 us -> 0 us
  between operations: 14.3 us -> 0.01 us
  local copies, waits for them, and re-layouts: 15.3 us -> 19.9 us
  other arithmetic: 3.99 us -> 0 us
    pallas_call x0 -> x1, Pallas kernels: none -> 88.6 us  [body(): pl.pallas_call(functools.partial(kernel, n), out_shape=jax.ShapeDtypeStru...]
    unnamed x1 -> x0, blocking collectives: 82.4 us -> none
    all_gather x1 -> x0, waiting for transfers between devices: 60.7 us -> none  [body(): lax.all_gather(hidden_in, 'tp', axis=0, tiled=True)]
    all_to_all x1 -> x0, blocking collectives: 27.4 us -> none  [body(): lax.all_to_all(send_rows, 'tp', split_axis=0, concat_axis=0, tiled=True)]
    all_to_all x1 -> x0, waiting for transfers between devices: 21.9 us -> none  [body(): lax.all_to_all(partial_out.reshape(devices, slot_count, feature_dim), 'tp...]
    dot_general x6 -> x0, matrix products: 20.2 us -> none  [the longest x1 9.17 us: body(): jnp.dot(inner_act, dense_down, preferred_element_type=jnp.float32)]
    unnamed x8 -> x0, starting transfers between devices: 19.4 us -> none
    unnamed x26 -> x5, local copies, waits for them, and re-layouts: 6.86 us -> 17.2 us
  transfers between devices with their start and end apart: 10 -> 0, of which waited for: 3 -> 0; matrix products, arithmetic and copies ran while one was open for 1% -> 0% of each run, Pallas kernels for 0% -> 0%
where the time goes in v1:
time: 109 us; the launch traced here: 108 us
  Pallas kernels  88.6 us (81%)
  local copies, waits for them, and re-layouts  19.9 us (18%)
    pallas_call x1, Pallas kernels, body(): pl.pallas_call(functools.partial(kernel, n), out_shape=jax.ShapeDtypeStru...  88.6 us
    unnamed x5, local copies, waits for them, and re-layouts  17.2 us

profile of v1, /device:TPU:0, one launch (start us, length us, event | category | flops | bytes accessed | tf_op | source)
XLA Modules:
  0.0 108.4 jit_solution(17042322731948651995)
XLA Ops:
  0.0 1.4 %copy.16.ids = s32[6,4]{1,0:T(8,128)} copy(s32[6,4]{0,1:T(4,128)} %param.22) | data formatting | bytes 192 | tf_op args[9]
  1.4 1.4 %copy.17.gws = f32[6,4]{1,0:T(8,128)} copy(f32[6,4]{0,1:T(4,128)} %param.23) | data formatting | bytes 192 | tf_op args[10]
  2.7 1.3 %reshape.12.gain1 = f32[1,3584]{1,0:T(1,128)} reshape(f32[3584]{0:T(1024)} %param.14) | data formatting | bytes 28672 | tf_op jit(solution)/shard_map/reshape | solution.py:345
  4.0 1.3 %reshape.13.gain2 = f32[1,3584]{1,0:T(1,128)} reshape(f32[3584]{0:T(1024)} %param.18) | data formatting | bytes 28672 | tf_op jit(solution)/shard_map/reshape | solution.py:349
  5.4 6.5 %copy.14.wg_hbm = bf16[3584,576]{1,0:T(8,128)(2,1)} copy(bf16[3584,576]{0,1:T(8,128)(2,1)} %param.15) | data formatting | bytes 8257536 | tf_op args[2]
  11.9 6.6 %copy.15.wu_hbm = bf16[3584,576]{1,0:T(8,128)(2,1)} copy(bf16[3584,576]{0,1:T(8,128)(2,1)} %param.16) | data formatting | bytes 8257536 | tf_op args[3]
  18.4 88.6 %shard_map.127 = bf16[6,3584]{1,0:T(8,128)(2,1)} custom-call(bf16[6,3584]{1,0:T(8,128)(2,1)} %hid.1, f32[1,3584]{1,0:T(1,128)} %reshape.12.gain1, bf16[3584,576]{1,0:T(8,128)(2,1)} %copy.14.wg_hbm, bf16[3584,576]{1,0:T(8,128)(2,1)} %copy.15.wu_hbm, bf16[576,3584]{1,0:T(8,128)(2,1)} %wd_hbm.1, f32[1,3584]{1,0:T(1,128)} %reshape.13.gain2, ...), custom_call_target="tpu_custom_call" | custom-call | tf_op jit(solution)/shard_map/pallas_call | solution.py:308
  107.0 1.4 %copy.19 = bf16[6,3584]{1,0:T(8,128)(2,1)} copy(bf16[6,3584]{1,0:T(8,128)(2,1)} %shard_map.127) | data formatting | bytes 86016

commit v2 on v1

--- a/solution.py
+++ b/solution.py
@@ -105,7 +105,7 @@
 
     hidden = hid[...].astype(jnp.float32)
     pad_ref[...] = jnp.zeros_like(pad_ref)
-    pad_ref[0:rows, :] = rms_scale(hidden, gain1[...])
+    pad_ref[0:rows, :] = rms_scale(hidden, gain1[...].reshape(1, D))
     buf1[0] = pad_ref[...].astype(jnp.bfloat16)
     pl.semaphore_wait(barrier, len(partners))
 
@@ -199,7 +199,7 @@
                 4 * PAD, D
             ).astype(jnp.bfloat16)
 
-    def project(gate_w, up_w, gate_acc, up_acc, result):
+    def project(gate_w, up_w, gate_acc, up_acc, result, columns):
         step = 512
         gate_acc[...] = jnp.zeros_like(gate_acc)
         up_acc[...] = jnp.zeros_like(up_acc)
@@ -208,8 +208,14 @@
         def _(i):
             span = pl.ds(pl.multiple_of(i * step, step), step)
             left = x2d[:, span]
-            gate_acc[...] += jnp.dot(left, gate_w[span, :], preferred_element_type=jnp.float32)
-            up_acc[...] += jnp.dot(left, up_w[span, :], preferred_element_type=jnp.float32)
+            for weight, total in ((gate_w, gate_acc), (up_w, up_acc)):
+                tile = weight[:, span] if columns else weight[span, :]
+                total[...] += lax.dot_general(
+                    left,
+                    tile,
+                    (((1,), (1 if columns else 0,)), ((), ())),
+                    preferred_element_type=jnp.float32,
+                )
 
         gate = gate_acc[...]
         result[...] = (gate / (1.0 + jnp.exp(-gate)) * up_acc[...]).astype(jnp.bfloat16)
@@ -228,7 +234,7 @@
     flatten(buf1)
     loads[0].wait()
     loads[1].wait()
-    project(wg, wu, acc_g, acc_u, inner)
+    project(wg, wu, acc_g, acc_u, inner, True)
     loads[2].wait()
     down(inner, wd, None)
     dense_sum = scatter(1, sbuf1, rbuf1)
@@ -236,30 +242,29 @@
     mixed = (hid[...].astype(jnp.float32) + dense_sum[0:rows]).astype(jnp.bfloat16)
     mixed = mixed.astype(jnp.float32)
     mixed_ref[...] = mixed
-    pad_ref[0:rows, :] = rms_scale(mixed, gain2[...])
+    pad_ref[0:rows, :] = rms_scale(mixed, gain2[...].reshape(1, D))
     buf2[0, :, 0:D] = pad_ref[...].astype(jnp.bfloat16)
-    lane = lax.broadcasted_iota(jnp.int32, (rows, LANES), 1)
+    lane = lax.broadcasted_iota(jnp.int32, (1, LANES), 1)
     expert = lax.rem(lane, HALF)
-    weight = jnp.zeros((rows, LANES), jnp.float32)
-    for k in range(TOP):
-        weight = weight + jnp.where(ids[:, k : k + 1] == expert, gws[:, k : k + 1], 0.0)
-    high = weight.astype(jnp.bfloat16).astype(jnp.float32)
-    pad_ref[0:rows, 0:LANES] = jnp.where(lane < HALF, high, weight - high)
+    for r in range(rows):
+        named = jnp.where(ids[:, r : r + 1] == expert, gws[:, r : r + 1], 0.0)
+        weight = jnp.sum(named, axis=0, keepdims=True)
+        high = weight.astype(jnp.bfloat16).astype(jnp.float32)
+        pad_ref[r : r + 1, 0:LANES] = jnp.where(lane < HALF, high, weight - high)
     buf2[0, :, D : D + LANES] = pad_ref[:, 0:LANES].astype(jnp.bfloat16)
 
     gather(2, buf2)
     flatten(buf2)
     loads[3].wait()
     loads[4].wait()
-    project(eg, eu, acc_eg, acc_eu, inner_e)
+    project(eg, eu, acc_eg, acc_eu, inner_e, False)
     slot = lax.broadcasted_iota(jnp.int32, (1, n), 1)
     hosted = jnp.sum(
         jnp.where(place[...] == me, lax.div(slot, SPLIT), 0).astype(jnp.float32),
         axis=1,
         keepdims=True,
     )
-    lane3 = lax.rem(lax.broadcasted_iota(jnp.int32, (1, LANES), 1), HALF)
-    chosen = jnp.where(lane3.astype(jnp.float32) == hosted, 1.0, 0.0)
+    chosen = jnp.where(expert.astype(jnp.float32) == hosted, 1.0, 0.0)
     row_weight = jnp.sum(
         buf2[:, :, D : D + LANES].astype(jnp.float32) * chosen[None], axis=2, keepdims=True
     )
@@ -311,8 +316,8 @@
         in_specs=[vmem, vmem, hbm, hbm, hbm, vmem, hbm, hbm, hbm, vmem, vmem, vmem, vmem],
         out_specs=vmem,
         scratch_shapes=[
-            pltpu.VMEM((D, F), bf16),
-            pltpu.VMEM((D, F), bf16),
+            pltpu.VMEM((F, D), bf16),
+            pltpu.VMEM((F, D), bf16),
             pltpu.VMEM((F, D), bf16),
             pltpu.VMEM((D, E), bf16),
             pltpu.VMEM((D, E), bf16),
@@ -342,16 +347,16 @@
         ),
     )(
         hidden_in,
-        norm_dense.reshape(1, D),
-        dense_gate,
-        dense_up,
+        norm_dense,
+        dense_gate.T,
+        dense_up.T,
         dense_down,
-        norm_moe.reshape(1, D),
+        norm_moe,
         expert_gate,
         expert_up,
         expert_down,
-        expert_ids,
-        gate_weights,
+        expert_ids.T,
+        gate_weights.T,
         placement.reshape(1, n),
         request_counts.reshape(1, n),
     )

time: 109 us -> 90.5 us (0.83)
  local copies, waits for them, and re-layouts: 19.9 us -> 1.45 us
    unnamed x5 -> x1, local copies, waits for them, and re-layouts: 17.2 us -> 1.45 us
    reshape x2 -> x0, local copies, waits for them, and re-layouts: 2.65 us -> none  [the longest x1 1.33 us: body(): norm_dense.reshape(1, D)]
where the time goes in v2:
time: 90.5 us; the launch traced here: 90.2 us
  Pallas kernels  88.8 us (98%)
  local copies, waits for them, and re-layouts  1.45 us (2%)
    pallas_call x1, Pallas kernels, body(): pl.pallas_call(functools.partial(kernel, n), out_shape=jax.ShapeDtypeStru...  88.8 us

profile of v2, /device:TPU:0, one launch (start us, length us, event | category | flops | bytes accessed | tf_op | source)
XLA Modules:
  0.0 90.2 jit_solution(7739086843535968904)
XLA Ops:
  0.0 88.8 %shard_map.127 = bf16[6,3584]{1,0:T(8,128)(2,1)} custom-call(bf16[6,3584]{1,0:T(8,128)(2,1)} %hid.1, f32[3584]{0:T(1024)} %gain1.1, bf16[576,3584]{1,0:T(8,128)(2,1)} %bitcast.6, bf16[576,3584]{1,0:T(8,128)(2,1)} %bitcast.7, bf16[576,3584]{1,0:T(8,128)(2,1)} %wd_hbm.1, f32[3584]{0:T(1024)} %gain2.1, bf16[1,3584,256]{2,1,0:T(8,128)(2,1)} %eg_hbm.1, ...), custom_call_target="tpu_custom_call" | custom-call | tf_op jit(solution)/shard_map/pallas_call | solution.py:313
  88.8 1.4 %copy.15 = bf16[6,3584]{1,0:T(8,128)(2,1)} copy(bf16[6,3584]{1,0:T(8,128)(2,1)} %shard_map.127) | data formatting | bytes 86016

commit v3 on v2

--- a/solution.py
+++ b/solution.py
@@ -49,8 +49,11 @@
     ed,
     pad_ref,
     mixed_ref,
-    buf1,
-    buf2,
+    sum_ref,
+    buf1a,
+    buf1b,
+    buf2a,
+    buf2b,
     x2d,
     acc_g,
     acc_u,
@@ -59,10 +62,14 @@
     acc_eu,
     inner_e,
     part,
-    sbuf1,
-    sbuf2,
-    rbuf1,
-    rbuf2,
+    sbuf1a,
+    sbuf1b,
+    sbuf2a,
+    sbuf2b,
+    rbuf1a,
+    rbuf1b,
+    rbuf2a,
+    rbuf2b,
     wsem,
     ssem,
     rsem,
@@ -70,6 +77,7 @@
     Z = n // 8
     rows = hid.shape[0]
     D = hid.shape[1]
+    W = D // 2
     me = lax.axis_index("tp")
     c = lax.rem(me, 2)
     x = lax.rem(lax.div(me, 2), 2)
@@ -106,98 +114,136 @@
     hidden = hid[...].astype(jnp.float32)
     pad_ref[...] = jnp.zeros_like(pad_ref)
     pad_ref[0:rows, :] = rms_scale(hidden, gain1[...].reshape(1, D))
-    buf1[0] = pad_ref[...].astype(jnp.bfloat16)
+    buf1a[0] = pad_ref[:, 0:W].astype(jnp.bfloat16)
+    buf1b[0] = pad_ref[:, W:D].astype(jnp.bfloat16)
     pl.semaphore_wait(barrier, len(partners))
 
-    def remote(phase, src, dst, k, dev):
+    def remote(phase, half, src, dst, k, dev):
         return pltpu.make_async_remote_copy(
             src_ref=src,
             dst_ref=dst,
-            send_sem=ssem.at[phase, k],
-            recv_sem=rsem.at[phase, k],
+            send_sem=ssem.at[phase, half],
+            recv_sem=rsem.at[phase, half, k],
             device_id={"tp": dev},
             device_id_type=pl.DeviceIdType.MESH,
         )
 
-    def gather(phase, buf):
-        def send(k, slot, dev):
-            remote(phase, buf.at[k], buf.at[slot], slot, dev).start()
-
-        def arrived(k):
-            remote(phase, buf.at[k], buf.at[k], k, c_dev).wait_recv()
-
-        send(0, 2 * Z, x_dev)
-        send(0, Z, y_dev)
+    steps = ((y_dev, x_dev), (x_dev, y_dev))
+
+    def place_of(half, group):
+        return group if half == 0 else (0, 2, 1, 3, 4, 6, 5, 7)[group]
+
+    def gather(phase, bufs):
+        def send(half, k, slot, dev):
+            buf = bufs[half]
+            remote(phase, half, buf.at[k], buf.at[slot], slot, dev).start()
+
+        def to_core(half, k):
+            buf = bufs[half]
+            remote(phase, half, buf.at[k], buf.at[4 * Z + k], 0, c_dev).start()
+
+        def arrived(half, k):
+            buf = bufs[half]
+            remote(phase, half, buf.at[k], buf.at[k], k, c_dev).wait_recv()
+
+        for half in range(2):
+            send(half, 0, 2 * Z, steps[half][1])
+            send(half, 0, Z, steps[half][0])
         for j in range(1, Z):
-            send(0, j, z_devs[j])
-        send(0, 4 * Z, c_dev)
+            for half in range(2):
+                send(half, 0, j, z_devs[j])
+        for half in range(2):
+            to_core(half, 0)
 
         @pl.loop(1, Z)
         def _(k):
-            arrived(k)
-            send(k, 2 * Z + k, x_dev)
-            send(k, Z + k, y_dev)
-            send(k, 4 * Z + k, c_dev)
+            for half in range(2):
+                arrived(half, k)
+                send(half, k, 2 * Z + k, steps[half][1])
+                send(half, k, Z + k, steps[half][0])
+                to_core(half, k)
 
         @pl.loop(Z, 2 * Z)
         def _(k):
-            arrived(k)
-            send(k, 2 * Z + k, x_dev)
-            send(k, 4 * Z + k, c_dev)
+            for half in range(2):
+                arrived(half, k)
+                send(half, k, 2 * Z + k, steps[half][1])
+                to_core(half, k)
 
         @pl.loop(2 * Z, 4 * Z)
         def _(k):
-            arrived(k)
-            send(k, 4 * Z + k, c_dev)
-
-        @pl.loop(4 * Z, 8 * Z)
-        def _(k):
-            arrived(k)
-
-    def scatter(phase, sbuf, rbuf):
-        def send(k, dev):
-            remote(phase, sbuf.at[k], rbuf.at[k], k, dev).start()
-
-        def arrived(k):
-            remote(phase, sbuf.at[k], rbuf.at[k], k, c_dev).wait_recv()
+            for half in range(2):
+                arrived(half, k)
+                to_core(half, k)
+
+        for half in range(2):
+            span = bufs[half].at[pl.ds(4 * Z, 4 * Z)]
+            remote(phase, half, span, span, 0, c_dev).wait_recv()
+
+    def open_scatter(phase, half, sbuf, rbuf):
+        base = half * W
+        for group in (7, 6, 5, 4):
+
+            @pl.loop(0, Z)
+            def _(i):
+                k = group * Z + (Z - 1 - i)
+                row = place_of(half, group) * Z + (Z - 1 - i)
+                sbuf[k] = part[row, :, base : base + W].astype(jnp.bfloat16)
+                remote(phase, half, sbuf.at[k], rbuf.at[k], k, c_dev).start()
+
+    def scatter(phase, sbufs, rbufs):
+        def send(half, k, dev):
+            sbuf, rbuf = sbufs[half], rbufs[half]
+            remote(phase, half, sbuf.at[k], rbuf.at[k], k, dev).start()
+
+        def arrived(half, k):
+            rbuf = rbufs[half]
+            remote(phase, half, rbuf.at[k], rbuf.at[k], k, c_dev).wait_recv()
             return rbuf[k].astype(jnp.float32)
 
-        def first(k):
-            sbuf[k] = part[k].astype(jnp.bfloat16)
-            send(k, c_dev)
-
-        pl.loop(6 * Z, 8 * Z)(first)
-        pl.loop(5 * Z, 6 * Z)(first)
-        pl.loop(4 * Z, 5 * Z)(first)
-
-        @pl.loop(2 * Z, 4 * Z)
-        def _(k):
-            total = part[k] + arrived(4 * Z + k)
-            sbuf[k] = total.astype(jnp.bfloat16)
-            send(k, x_dev)
-
-        @pl.loop(Z, 2 * Z)
-        def _(k):
-            total = part[k] + arrived(4 * Z + k) + arrived(2 * Z + k)
-            sbuf[k] = total.astype(jnp.bfloat16)
-            send(k, y_dev)
-
-        for k in range(1, Z):
-            total = part[k] + arrived(4 * Z + k) + arrived(2 * Z + k) + arrived(Z + k)
-            sbuf[k] = total.astype(jnp.bfloat16)
-            send(k, z_devs[Z - k])
-        total = part[0] + arrived(4 * Z) + arrived(2 * Z) + arrived(Z)
-        for k in range(1, Z):
-            total = total + arrived(k)
-        return total
-
-    def flatten(buf):
-        @pl.loop(0, n // 4)
-        def _(b):
-            block = buf[pl.ds(b * 4, 4), :, 0:D].astype(jnp.float32)
-            x2d[pl.ds(pl.multiple_of(b * 4 * PAD, 4 * PAD), 4 * PAD), :] = block.reshape(
-                4 * PAD, D
-            ).astype(jnp.bfloat16)
+        def own(half, group, i):
+            return part[place_of(half, group) * Z + i, :, half * W : half * W + W]
+
+        for group in (3, 2):
+
+            @pl.loop(0, Z)
+            def _(i):
+                j = Z - 1 - i
+                k = group * Z + j
+                for half in range(2):
+                    total = own(half, group, j) + arrived(half, 4 * Z + k)
+                    sbufs[half][k] = total.astype(jnp.bfloat16)
+                    send(half, k, steps[half][1])
+
+        @pl.loop(0, Z)
+        def _(i):
+            j = Z - 1 - i
+            k = Z + j
+            for half in range(2):
+                total = own(half, 1, j) + arrived(half, 4 * Z + k) + arrived(half, 2 * Z + k)
+                sbufs[half][k] = total.astype(jnp.bfloat16)
+                send(half, k, steps[half][0])
+
+        for k in reversed(range(1, Z)):
+            for half in range(2):
+                total = own(half, 0, k) + arrived(half, 4 * Z + k)
+                total = total + arrived(half, 2 * Z + k) + arrived(half, Z + k)
+                sbufs[half][k] = total.astype(jnp.bfloat16)
+                send(half, k, z_devs[Z - k])
+        for half in range(2):
+            total = own(half, 0, 0)
+            for k in (4 * Z, 2 * Z, Z) + tuple(reversed(range(1, Z))):
+                total = total + arrived(half, k)
+            sum_ref[:, half * W : half * W + W] = total
+
+    def flatten(bufs):
+        for half in range(2):
+            for group in range(8):
+                block = bufs[half][group * Z : group * Z + Z, :, 0:W].astype(jnp.float32)
+                row = place_of(half, group) * Z * PAD
+                x2d[row : row + Z * PAD, half * W : half * W + W] = block.reshape(
+                    Z * PAD, W
+                ).astype(jnp.bfloat16)
 
     def project(gate_w, up_w, gate_acc, up_acc, result, columns):
         step = 512
@@ -220,30 +266,36 @@
         gate = gate_acc[...]
         result[...] = (gate / (1.0 + jnp.exp(-gate)) * up_acc[...]).astype(jnp.bfloat16)
 
-    def down(act, down_w, scale):
-        step = 512
-
-        @pl.loop(0, D // step)
+    def down(act, down_w, scale, half):
+        step = 256
+
+        @pl.loop(0, W // step)
         def _(i):
-            span = pl.ds(pl.multiple_of(i * step, step), step)
+            span = pl.ds(pl.multiple_of(half * W + i * step, step), step)
             value = jnp.dot(act[...], down_w[:, span], preferred_element_type=jnp.float32)
             value = value.reshape(n, PAD, step)
             part[:, :, span] = value if scale is None else value * scale
 
+    buf1, buf2 = (buf1a, buf1b), (buf2a, buf2b)
+    sbuf1, sbuf2 = (sbuf1a, sbuf1b), (sbuf2a, sbuf2b)
+    rbuf1, rbuf2 = (rbuf1a, rbuf1b), (rbuf2a, rbuf2b)
     gather(0, buf1)
     flatten(buf1)
     loads[0].wait()
     loads[1].wait()
     project(wg, wu, acc_g, acc_u, inner, True)
     loads[2].wait()
-    down(inner, wd, None)
-    dense_sum = scatter(1, sbuf1, rbuf1)
-
-    mixed = (hid[...].astype(jnp.float32) + dense_sum[0:rows]).astype(jnp.bfloat16)
+    for half in range(2):
+        down(inner, wd, None, half)
+        open_scatter(1, half, sbuf1[half], rbuf1[half])
+    scatter(1, sbuf1, rbuf1)
+
+    mixed = (hid[...].astype(jnp.float32) + sum_ref[0:rows, :]).astype(jnp.bfloat16)
     mixed = mixed.astype(jnp.float32)
     mixed_ref[...] = mixed
     pad_ref[0:rows, :] = rms_scale(mixed, gain2[...].reshape(1, D))
-    buf2[0, :, 0:D] = pad_ref[...].astype(jnp.bfloat16)
+    buf2a[0, :, 0:W] = pad_ref[:, 0:W].astype(jnp.bfloat16)
+    buf2b[0] = pad_ref[:, W:D].astype(jnp.bfloat16)
     lane = lax.broadcasted_iota(jnp.int32, (1, LANES), 1)
     expert = lax.rem(lane, HALF)
     for r in range(rows):
@@ -251,7 +303,7 @@
         weight = jnp.sum(named, axis=0, keepdims=True)
         high = weight.astype(jnp.bfloat16).astype(jnp.float32)
         pad_ref[r : r + 1, 0:LANES] = jnp.where(lane < HALF, high, weight - high)
-    buf2[0, :, D : D + LANES] = pad_ref[:, 0:LANES].astype(jnp.bfloat16)
+    buf2a[0, :, W : W + LANES] = pad_ref[:, 0:LANES].astype(jnp.bfloat16)
 
     gather(2, buf2)
     flatten(buf2)
@@ -266,25 +318,25 @@
     )
     chosen = jnp.where(expert.astype(jnp.float32) == hosted, 1.0, 0.0)
     row_weight = jnp.sum(
-        buf2[:, :, D : D + LANES].astype(jnp.float32) * chosen[None], axis=2, keepdims=True
+        buf2a[:, :, W : W + LANES].astype(jnp.float32) * chosen[None], axis=2, keepdims=True
     )
     loads[5].wait()
-    down(inner_e, ed, row_weight)
-    routed_sum = scatter(3, sbuf2, rbuf2)
+    for half in range(2):
+        down(inner_e, ed, row_weight, half)
+        open_scatter(3, half, sbuf2[half], rbuf2[half])
+    scatter(3, sbuf2, rbuf2)
 
     count = jnp.sum(
         jnp.where(slot == me, counts[...], 0).astype(jnp.float32), axis=1, keepdims=True
     )
     row = lax.broadcasted_iota(jnp.int32, (rows, 1), 0).astype(jnp.float32)
-    final = mixed_ref[...] + routed_sum[0:rows]
+    final = mixed_ref[...] + sum_ref[0:rows, :]
     out[...] = jnp.where(row < DRAFT * count, final, 0.0).astype(out.dtype)
 
-    @pl.loop(1, n)
-    def _(k):
-        remote(0, buf1.at[k], buf1.at[k], k, c_dev).wait_send()
-        remote(1, sbuf1.at[k], rbuf1.at[k], k, c_dev).wait_send()
-        remote(2, buf2.at[k], buf2.at[k], k, c_dev).wait_send()
-        remote(3, sbuf2.at[k], rbuf2.at[k], k, c_dev).wait_send()
+    for phase, sent in enumerate((buf1, sbuf1, buf2, sbuf2)):
+        for half in range(2):
+            span = sent[half].at[pl.ds(1, n - 1)]
+            remote(phase, half, span, span, 0, c_dev).wait_send()
 
 
 def body(
@@ -324,8 +376,11 @@
             pltpu.VMEM((E, D), bf16),
             pltpu.VMEM((PAD, D), f32),
             pltpu.VMEM(hidden_in.shape, f32),
-            pltpu.VMEM((n, PAD, D), bf16),
-            pltpu.VMEM((n, PAD, D + LANES), bf16),
+            pltpu.VMEM((PAD, D), f32),
+            pltpu.VMEM((n, PAD, D // 2), bf16),
+            pltpu.VMEM((n, PAD, D // 2), bf16),
+            pltpu.VMEM((n, PAD, D // 2 + LANES), bf16),
+            pltpu.VMEM((n, PAD, D // 2), bf16),
             pltpu.VMEM((total_rows, D), bf16),
             pltpu.VMEM((total_rows, F), f32),
             pltpu.VMEM((total_rows, F), f32),
@@ -334,13 +389,10 @@
             pltpu.VMEM((total_rows, E), f32),
             pltpu.VMEM((total_rows, E), bf16),
             pltpu.VMEM((n, PAD, D), f32),
-            pltpu.VMEM((n, PAD, D), bf16),
-            pltpu.VMEM((n, PAD, D), bf16),
-            pltpu.VMEM((n, PAD, D), bf16),
-            pltpu.VMEM((n, PAD, D), bf16),
+            *[pltpu.VMEM((n, PAD, D // 2), bf16)] * 8,
             pltpu.SemaphoreType.DMA((6,)),
-            pltpu.SemaphoreType.DMA((4, n)),
-            pltpu.SemaphoreType.DMA((4, n)),
+            pltpu.SemaphoreType.DMA((4, 2)),
+            pltpu.SemaphoreType.DMA((4, 2, n)),
         ],
         compiler_params=pltpu.CompilerParams(
             collective_id=0, has_side_effects=True, vmem_limit_bytes=60 * 1024 * 1024

time: 90.5 us -> 78.2 us (0.86)
  Pallas kernels: 88.8 us -> 76.6 us
    pallas_call x1, Pallas kernels: 88.8 us -> 76.6 us  [body(): pl.pallas_call(functools.partial(kernel, n), out_shape=jax.ShapeDtypeStru...]
where the time goes in v3:
time: 78.2 us; the launch traced here: 78 us
  Pallas kernels  76.6 us (98%)
  local copies, waits for them, and re-layouts  1.45 us (2%)
    pallas_call x1, Pallas kernels, body(): pl.pallas_call(functools.partial(kernel, n), out_shape=jax.ShapeDtypeStru...  76.6 us

profile of v3, /device:TPU:0, one launch (start us, length us, event | category | flops | bytes accessed | tf_op | source)
XLA Modules:
  0.0 78.0 jit_solution(11849619314268532688)
XLA Ops:
  0.0 76.6 %shard_map.127 = bf16[6,3584]{1,0:T(8,128)(2,1)} custom-call(bf16[6,3584]{1,0:T(8,128)(2,1)} %hid.1, f32[3584]{0:T(1024)} %gain1.1, bf16[576,3584]{1,0:T(8,128)(2,1)} %bitcast.6, bf16[576,3584]{1,0:T(8,128)(2,1)} %bitcast.7, bf16[576,3584]{1,0:T(8,128)(2,1)} %wd_hbm.1, f32[3584]{0:T(1024)} %gain2.1, bf16[1,3584,256]{2,1,0:T(8,128)(2,1)} %eg_hbm.1, ...), custom_call_target="tpu_custom_call" | custom-call | tf_op jit(solution)/shard_map/pallas_call | solution.py:365
  76.6 1.4 %copy.15 = bf16[6,3584]{1,0:T(8,128)(2,1)} copy(bf16[6,3584]{1,0:T(8,128)(2,1)} %shard_map.127) | data formatting | bytes 86016

commit v4 on v3

--- a/solution.py
+++ b/solution.py
@@ -176,10 +176,6 @@
                 arrived(half, k)
                 to_core(half, k)
 
-        for half in range(2):
-            span = bufs[half].at[pl.ds(4 * Z, 4 * Z)]
-            remote(phase, half, span, span, 0, c_dev).wait_recv()
-
     def open_scatter(phase, half, sbuf, rbuf):
         base = half * W
         for group in (7, 6, 5, 4):
@@ -236,14 +232,18 @@
                 total = total + arrived(half, k)
             sum_ref[:, half * W : half * W + W] = total
 
-    def flatten(bufs):
-        for half in range(2):
-            for group in range(8):
-                block = bufs[half][group * Z : group * Z + Z, :, 0:W].astype(jnp.float32)
-                row = place_of(half, group) * Z * PAD
-                x2d[row : row + Z * PAD, half * W : half * W + W] = block.reshape(
-                    Z * PAD, W
-                ).astype(jnp.bfloat16)
+    def flatten(phase, bufs):
+        for late in range(2):
+            for half in range(2):
+                if late:
+                    span = bufs[half].at[pl.ds(4 * Z, 4 * Z)]
+                    remote(phase, half, span, span, 0, c_dev).wait_recv()
+                for group in range(4 * late, 4 * late + 4):
+                    block = bufs[half][group * Z : group * Z + Z, :, 0:W].astype(jnp.float32)
+                    row = place_of(half, group) * Z * PAD
+                    x2d[row : row + Z * PAD, half * W : half * W + W] = block.reshape(
+                        Z * PAD, W
+                    ).astype(jnp.bfloat16)
 
     def project(gate_w, up_w, gate_acc, up_acc, result, columns):
         step = 512
@@ -280,7 +280,7 @@
     sbuf1, sbuf2 = (sbuf1a, sbuf1b), (sbuf2a, sbuf2b)
     rbuf1, rbuf2 = (rbuf1a, rbuf1b), (rbuf2a, rbuf2b)
     gather(0, buf1)
-    flatten(buf1)
+    flatten(0, buf1)
     loads[0].wait()
     loads[1].wait()
     project(wg, wu, acc_g, acc_u, inner, True)
@@ -306,7 +306,7 @@
     buf2a[0, :, W : W + LANES] = pad_ref[:, 0:LANES].astype(jnp.bfloat16)
 
     gather(2, buf2)
-    flatten(buf2)
+    flatten(2, buf2)
     loads[3].wait()
     loads[4].wait()
     project(eg, eu, acc_eg, acc_eu, inner_e, False)

time: 78.2 us -> 78 us (level)
  no operation moved by 1% of the time
where the time goes in v4:
time: 78 us; the launch traced here: 77.8 us
  Pallas kernels  76.4 us (98%)
  local copies, waits for them, and re-layouts  1.45 us (2%)
    pallas_call x1, Pallas kernels, body(): pl.pallas_call(functools.partial(kernel, n), out_shape=jax.ShapeDtypeStru...  76.4 us

profile of v4, /device:TPU:0, one launch (start us, length us, event | category | flops | bytes accessed | tf_op | source)
XLA Modules:
  0.0 77.8 jit_solution(17130975778987574193)
XLA Ops:
  0.0 76.4 %shard_map.127 = bf16[6,3584]{1,0:T(8,128)(2,1)} custom-call(bf16[6,3584]{1,0:T(8,128)(2,1)} %hid.1, f32[3584]{0:T(1024)} %gain1.1, bf16[576,3584]{1,0:T(8,128)(2,1)} %bitcast.6, bf16[576,3584]{1,0:T(8,128)(2,1)} %bitcast.7, bf16[576,3584]{1,0:T(8,128)(2,1)} %wd_hbm.1, f32[3584]{0:T(1024)} %gain2.1, bf16[1,3584,256]{2,1,0:T(8,128)(2,1)} %eg_hbm.1, ...), custom_call_target="tpu_custom_call" | custom-call | tf_op jit(solution)/shard_map/pallas_call | solution.py:365
  76.4 1.4 %copy.15 = bf16[6,3584]{1,0:T(8,128)(2,1)} copy(bf16[6,3584]{1,0:T(8,128)(2,1)} %shard_map.127) | data formatting | bytes 86016
